TPU v7x, 512 devices: a whole 4x8x8 slice. The times are simulated.
512 devices in a mesh: tm: 16 (over y, core), nin: 8 (over z), nout: 4 (over x).
Axes of the slice: x: 4, y: 8, z: 8, core: 2. Of those that a mesh axis runs over, the one named last changes fastest.
Arguments:
- spikes: int32 [4096, 2048], P('tm', 'nin'), may hold values 0 or 1
- exposure: int32 [4096], P('tm'), may hold values from 1 to 8
- weights: bfloat16 [16384, 2048], P('nin', 'nout'), may hold values from -0.375 to 0.375
- direction: float32 [16384, 2048], P(('nin', 'tm'), 'nout'), may hold values from -6 to 6
- residual: float32 [16384, 2048], P(('nin', 'tm'), 'nout'), may hold values from -0.75 to 0.75
- iterate: float32 [16384, 2048], P(('nin', 'tm'), 'nout'), may hold values from -1.8 to 1.8
Outputs:
- new_iterate: float32 [16384, 2048], P(('nin', 'tm'), 'nout')
- new_residual: float32 [16384, 2048], P(('nin', 'tm'), 'nout')
- new_direction: float32 [16384, 2048], P(('nin', 'tm'), 'nout')
All inputs are finite; a program needn't handle non-finite values. No bound on the sum of `spikes` on one device may be relied on, other than what follows from the above.
Results may differ from a plain program's by a relative error of at most 0.015.
Values may be sent and summed in bfloat16 or wider, within the bound.
A program may use at most 64 MiB of HBM per device.

v0:
```python
import math
import jax
import jax.numpy as jnp
from jax import lax
from jax.sharding import PartitionSpec as P

BASES = 8
HISTORY = 128
RIDGE_WEIGHT = 0.05
NORM_EPS = 1e-06


def shifted(value, axis, steps):
    count = lax.axis_size(axis)
    initial, last = (max(0, -steps), min(count, count - steps))
    return lax.ppermute(value, axis, [(source, source + steps) for source in range(initial, last)])


def basis_table(history, bases_count):
    lag_values = jnp.arange(1, history + 1, dtype=jnp.float32)
    warped = jnp.log(lag_values + 1.0)
    log_low = math.log(2.0)
    log_high = math.log(history + 1.0)
    spacing = (log_high - log_low) / (bases_count - 1)
    centers = log_low + spacing * jnp.arange(bases_count, dtype=jnp.float32)
    phases = (warped[:, None] - centers[None, :]) * (math.pi / (2.0 * spacing))
    phases = jnp.clip(phases, -math.pi, math.pi)
    bump_values = 0.5 * (1.0 + jnp.cos(phases))
    bump_values = bump_values / jnp.sum(bump_values, axis=0, keepdims=True)
    return bump_values.astype(jnp.bfloat16)


def lag_kernel(basis_rows, span, offset):
    out_index = jnp.arange(span, dtype=jnp.int32)[:, None]
    in_index = jnp.arange(span, dtype=jnp.int32)[None, :]
    lag_index = out_index + offset - in_index
    is_valid = (lag_index >= 1) & (lag_index <= HISTORY)
    take_index = jnp.clip(lag_index - 1, 0, HISTORY - 1)
    return jnp.where(
        is_valid[None], jnp.take(basis_rows.T, take_index, axis=1), jnp.zeros((), jnp.bfloat16)
    )


def per_device(spikes, exposure, weights, direction, residual, iterate):
    block_rows = spikes.shape[0]
    neuron_cols = spikes.shape[1]
    basis_rows = basis_table(HISTORY, BASES)
    spike_low = spikes.astype(jnp.bfloat16)
    block_count = block_rows // HISTORY
    stacked = spike_low.reshape(block_count, HISTORY, neuron_cols)
    kernel_same = lag_kernel(basis_rows, HISTORY, 0)
    kernel_before = lag_kernel(basis_rows, HISTORY, HISTORY)
    current = jnp.einsum("bim,cmn->cinb", kernel_same, stacked, preferred_element_type=jnp.float32)
    tail_part = jnp.einsum(
        "bim,mn->inb", kernel_before, stacked[-1], preferred_element_type=jnp.float32
    )
    inner_part = jnp.einsum(
        "bim,cmn->cinb", kernel_before, stacked[:-1], preferred_element_type=jnp.float32
    )
    tail_terms = shifted(tail_part.astype(jnp.bfloat16), "tm", 1).astype(tail_part.dtype)
    own_terms = current + jnp.concatenate([tail_terms[None], inner_part], axis=0)
    features = own_terms.reshape(block_rows, neuron_cols * BASES).astype(jnp.bfloat16)
    direction_low = direction.astype(jnp.bfloat16)
    columns = features
    along_part = jnp.dot(
        columns,
        lax.all_gather(direction_low, "tm", axis=0, tiled=True),
        preferred_element_type=jnp.float32,
    )
    predictor_part = jnp.dot(features, weights, preferred_element_type=jnp.float32)
    tick_scale = exposure.astype(jnp.float32) / 8.0
    predictor_full, along_full = (
        lax.psum(predictor_part.astype(jnp.bfloat16), "nin").astype(jnp.float32),
        lax.psum(along_part.astype(jnp.bfloat16), "nin").astype(jnp.float32),
    )
    weighted = (tick_scale[:, None] * jnp.exp(predictor_full) * along_full).astype(jnp.bfloat16)
    columns = features
    gram = lax.psum_scatter(
        lax.dot_general(
            columns, weighted, (((0,), (0,)), ((), ())), preferred_element_type=jnp.float32
        ).astype(jnp.bfloat16),
        "tm",
        scatter_dimension=0,
        tiled=True,
    ).astype(jnp.float32)
    bin_total = block_rows * lax.axis_size("tm")
    curvature_prod = gram / bin_total + RIDGE_WEIGHT * direction
    old_norm, curvature = lax.psum(
        (jnp.sum(residual * residual, axis=0), jnp.sum(direction * curvature_prod, axis=0)),
        ("tm", "nin"),
    )
    step_size = old_norm / curvature
    new_iterate = iterate + step_size[None, :] * direction
    new_residual = residual - step_size[None, :] * curvature_prod
    new_norm = lax.psum(jnp.sum(new_residual * new_residual, axis=0), ("tm", "nin"))
    new_direction = new_residual + (new_norm / (old_norm + NORM_EPS))[None, :] * direction
    return (new_iterate, new_residual, new_direction)


def solution(mesh):
    in_specs = (
        P("tm", "nin"),
        P("tm"),
        P("nin", "nout"),
        P(("nin", "tm"), "nout"),
        P(("nin", "tm"), "nout"),
        P(("nin", "tm"), "nout"),
    )
    out_specs = (P(("nin", "tm"), "nout"), P(("nin", "tm"), "nout"), P(("nin", "tm"), "nout"))
    return jax.shard_map(
        per_device, mesh=mesh, in_specs=in_specs, out_specs=out_specs, check_vma=False
    )
```

profile of v0, /device:TPU:2, one launch (start us, length us, event | category | flops | bytes accessed | tf_op | source)
XLA Modules:
  0.0 800.1 jit_solution(18235166921538115580)
XLA Ops:
  7.2 0.0 all-gather.2.cloned.1.call-start
  7.2 1.8 convert_element_type.56
  9.0 0.0 all-gather.2.cloned.1.call-update
  9.0 0.0 all-reduce.4.cloned.1.call-start
  9.1 0.2 multiply_reduce_fusion.3
  9.3 0.1 divide_convert_fusion
  9.4 0.1 copy.17
  9.6 0.1 bitcast_clamp_fusion
  9.7 57.8 %gather_fusion.1 = bf16[16384,8]{1,0:T(8,128)(2,1)} fusion(bf16[8,128]{0,1:T(8,128)(2,1)S(1)} %copy.17, s32[16384]{0:T(1024)S(1)} %bitcast_clamp_fusion), kind=kCustom, calls=%fused_computation.1.clone | custom fusion | bytes 589824 | tf_op jit(solution)/shard_map/jit(_take)/gather | solution.py:40
  67.5 3.6 copy.20
  71.2 0.1 fusion.30
  71.3 1.1 fusion.1
  72.4 1.8 collective-permute-start
  74.2 57.8 %gather_fusion = bf16[16384,8]{1,0:T(8,128)(2,1)} fusion(bf16[8,128]{0,1:T(8,128)(2,1)S(1)} %copy.17, s32[16384]{0:T(1024)S(1)} %bitcast_clamp_fusion.1), kind=kCustom, calls=%fused_computation.clone | custom fusion | bytes 589824 | tf_op jit(solution)/shard_map/jit(_take)/gather | solution.py:40
  132.0 3.6 copy.18
  135.6 0.1 fusion.27
  135.7 0.3 convolution_bitcast_fusion
  136.0 0.1 bitcast_convert_fusion
  136.1 0.4 fusion
  136.5 2.1 copy.21
  138.6 2.8 convolution_convert_fusion.3
  141.4 3.0 convolution_convert_fusion.2
  144.4 0.0 all-reduce.4.cloned.1.call-update
  144.5 0.0 reduce-scatter.2.cloned.1.call-start
  144.5 85.0 %all-reduce.4.cloned.1.call-done = (bf16[256,512]{1,0:T(8,128)(2,1)}, bf16[256,512]{1,0:T(8,128)(2,1)}) async-done(((bf16[256,512]{1,0:T(8,128)(2,1)}, bf16[256,512]{1,0:T(8,128)(2,1)}), (bf16[256,512]{1,0:T(8,128)(2,1)}, bf16[256,512]{1,0:T(8,128)(2,1)})) %all-reduce.4.cloned.1.call-update) | async-done | bytes 524304 | tf_op jit(solution)/shard_map/psum | solution.py:74
  229.5 3.2 convolution_convert_fusion
  232.9 59.8 %reduce-scatter.2.cloned.1.call-done = bf16[128,512]{1,0:T(8,128)(2,1)} async-done(((bf16[2048,512]{1,0:T(8,128)(2,1)}), bf16[128,512]{1,0:T(8,128)(2,1)}) %reduce-scatter.2.cloned.1.call-update) | async-done | bytes 131088 | tf_op jit(solution)/shard_map/reduce_scatter | solution.py:78
  292.7 1.0 multiply_reduce_fusion.1
  293.6 250.6 %all-reduce = (f32[512]{0:T(512)S(1)}, f32[512]{0:T(512)S(1)}) all-reduce(f32[512]{0:T(512)S(1)} %multiply_reduce_fusion.2, f32[512]{0:T(512)S(1)} %multiply_reduce_fusion.1), channel_id=1, replica_groups=mesh['tm'=16,'nin'=8,'nout'=4] {'tm','nin'}, use_global_device_ids=true, to_apply=%region_1.2 | all-reduce | flops 1024 | bytes 8192 | tf_op jit(solution)/shard_map/psum | solution.py:88
  544.3 1.7 multiply_reduce_fusion
  546.0 246.8 %psum.39 = f32[512]{0:T(512)S(1)} all-reduce(f32[512]{0:T(512)S(1)} %get-tuple-element.8), channel_id=1, replica_groups=mesh['tm'=16,'nin'=8,'nout'=4] {'tm','nin'}, use_global_device_ids=true, to_apply=%region_9.11 | all-reduce | flops 512 | bytes 4096 | tf_op jit(solution)/shard_map/psum | solution.py:95
  792.8 0.8 multiply_add_fusion
  (28 shorter events, 0.2 us)
Async XLA Ops:
  7.2 131.5 %copy-start = (bf16[2048,512]{1,0:T(8,128)(2,1)S(1)}, bf16[2048,512]{1,0:T(8,128)(2,1)}, u32[]{:S(2)}) copy-start(bf16[2048,512]{1,0:T(8,128)(2,1)} %param.10) | copy-start | bytes 6291460
  7.2 134.2 %all-gather.2.cloned.1.call-start = ((), (), s32[]{:S(2)}) async-start(), calls=%async_computation.1 | async-start | bytes 2228224 | tf_op jit(solution)/shard_map/all_gather | solution.py:67
  9.0 220.5 %all-reduce.4.cloned.1.call-start = ((), (), s32[]{:S(2)}) async-start(), calls=%async_computation.3 | async-start | bytes 1048576 | tf_op jit(solution)/shard_map/psum | solution.py:74
  67.5 3.6 copy-start.5
  72.4 63.6 %collective-permute-start = (bf16[128,256,8]{1,0,2:T(8,128)(2,1)}, bf16[128,256,8]{1,0,2:T(8,128)(2,1)S(1)}, u32[]{:S(2)}, u32[]{:S(2)}) collective-permute-start(bf16[128,256,8]{1,0,2:T(8,128)(2,1)} %fusion.1), channel_id=1, source_target_pairs={{0,32},{32,64},{64,96},{96,128},{128,160},{160,192},{192,224},{224... | collective-permute-start | bytes 1572872 | tf_op jit(solution)/shard_map/ppermute | solution.py:16
  138.6 2.8 copy-start.2
  141.4 3.1 copy-start.7
  144.5 148.2 %reduce-scatter.2.cloned.1.call-start = ((), (), s32[]{:S(2)}) async-start(), calls=%async_computation.2 | async-start | bytes 2228224 | tf_op jit(solution)/shard_map/reduce_scatter | solution.py:78
  229.5 3.3 copy-start.4
  232.8 59.9 %copy-start.1 = (f32[128,512]{1,0:T(8,128)S(1)}, f32[128,512]{1,0:T(8,128)}, u32[]{:S(2)}) copy-start(f32[128,512]{1,0:T(8,128)} %param.11) | copy-start | bytes 786436
  232.8 311.5 %copy-start.6 = (f32[128,512]{1,0:T(8,128)S(1)}, f32[128,512]{1,0:T(8,128)}, u32[]{:S(2)}) copy-start(f32[128,512]{1,0:T(8,128)} %param.13) | copy-start | bytes 786436
  546.0 247.6 %copy-start.3 = (f32[128,512]{1,0:T(8,128)}, f32[128,512]{1,0:T(8,128)S(1)}, u32[]{:S(2)}) copy-start(f32[128,512]{1,0:T(8,128)S(1)} %get-tuple-element.9) | copy-start | bytes 786436
Sparse Core Ops, SparseCore 0:
  10.7 46.5 all-gather.1
  144.6 84.9 all-reduce.3
  232.9 59.6 reduce-scatter.1
where the time goes:
time: 800 us
  blocking collectives  497 us (62%)
  waiting for transfers between devices  145 us (18%)
  local copies, waits for them, and re-layouts  125 us (16%)
  between operations  13.9 us (2%)
  matrix products  10.8 us (1%)
    psum x1, blocking collectives, per_device(): lax.psum((jnp.sum(residual * residual, axis=0), jnp.sum(direction * curva...  251 us
    psum x1, blocking collectives, per_device(): lax.psum(jnp.sum(new_residual * new_residual, axis=0), ('tm', 'nin'))  247 us
    gather x4, local copies, waits for them, and re-layouts, lag_kernel(): jnp.take(basis_rows.T, take_index, axis=1)  123 us
    psum x1, waiting for transfers between devices, per_device(): lax.psum(along_part.astype(jnp.bfloat16), 'nin').astype(jnp.float32)  85 us
    reduce_scatter x1, waiting for transfers between devices, per_device(): lax.psum_scatter(lax.dot_general(columns, weighted, (((0,), (0,)), ((), (...  59.8 us
  transfers between devices with their start and end apart: 4, of which 2 were waited for; matrix products, arithmetic and copies ran while one was open for 16% of the time, Pallas kernels for 0%

commit v1 on v0

--- a/solution.py
+++ b/solution.py
@@ -1,3 +1,4 @@
+import functools
 import math
 import jax
 import jax.numpy as jnp
@@ -8,6 +9,14 @@
 HISTORY = 128
 RIDGE_WEIGHT = 0.05
 NORM_EPS = 1e-06
+
+
+def group_column_by_axis(in_array, device_axis, lane_axis):
+    state_next = lax.psum(lax.psum(in_array, axis_name=device_axis), axis_name=lane_axis)
+    return state_next
+
+
+_name_edges = functools.partial(group_column_by_axis, device_axis="nin", lane_axis="tm")
 
 
 def shifted(value, axis, steps):
@@ -85,9 +94,8 @@
     ).astype(jnp.float32)
     bin_total = block_rows * lax.axis_size("tm")
     curvature_prod = gram / bin_total + RIDGE_WEIGHT * direction
-    old_norm, curvature = lax.psum(
-        (jnp.sum(residual * residual, axis=0), jnp.sum(direction * curvature_prod, axis=0)),
-        ("tm", "nin"),
+    old_norm, curvature = _name_edges(
+        (jnp.sum(residual * residual, axis=0), jnp.sum(direction * curvature_prod, axis=0))
     )
     step_size = old_norm / curvature
     new_iterate = iterate + step_size[None, :] * direction

time: 800 us -> 591 us (0.74)
  blocking collectives: 497 us -> 288 us
    psum x1 -> x2, blocking collectives: 251 us -> 41.6 us  [the longest x1 23.5 us: group_column_by_axis(): lax.psum(lax.psum(in_array, axis_name=device_axis), axis_name=lane_axis)]
  transfers between devices with their start and end apart: 4 -> 4, of which waited for: 2 -> 2; matrix products, arithmetic and copies ran while one was open for 16% -> 22% of each run, Pallas kernels for 0% -> 0%
where the time goes in v1:
time: 591 us; the launch traced here: 590 us
  blocking collectives  288 us (49%)
  waiting for transfers between devices  145 us (25%)
  local copies, waits for them, and re-layouts  124 us (21%)
  between operations  13.9 us (2%)
  matrix products  10.8 us (2%)
  other arithmetic  6.02 us (1%)
    psum x1, blocking collectives, per_device(): lax.psum(jnp.sum(new_residual * new_residual, axis=0), ('tm', 'nin'))  247 us
    gather x4, local copies, waits for them, and re-layouts, lag_kernel(): jnp.take(basis_rows.T, take_index, axis=1)  122 us
    psum x1, waiting for transfers between devices, per_device(): lax.psum(along_part.astype(jnp.bfloat16), 'nin').astype(jnp.float32)  85 us
    reduce_scatter x1, waiting for transfers between devices, per_device(): lax.psum_scatter(lax.dot_general(columns, weighted, (((0,), (0,)), ((), (...  59.8 us
    psum x1, blocking collectives, group_column_by_axis(): lax.psum(lax.psum(in_array, axis_name=device_axis), axis_name=lane_axis)  23.5 us
    psum x1, blocking collectives, group_column_by_axis(): lax.psum(in_array, axis_name=device_axis)  18.1 us
  transfers between devices with their start and end apart: 4, of which 2 were waited for; matrix products, arithmetic and copies ran while one was open for 22% of the time, Pallas kernels for 0%

profile of v1, /device:TPU:2, one launch (start us, length us, event | category | flops | bytes accessed | tf_op | source)
XLA Modules:
  0.0 590.2 jit_solution(10912039187463895162)
XLA Ops:
  7.2 0.0 all-gather.2.cloned.1.call-start
  7.2 1.8 convert_element_type.56
  9.0 0.0 all-reduce.5.cloned.1.call-start
  9.1 0.2 multiply_reduce_fusion.3
  9.3 0.1 divide_convert_fusion
  9.4 0.1 copy.17
  9.6 0.1 bitcast_clamp_fusion
  9.7 57.4 %gather_fusion.1 = bf16[16384,8]{1,0:T(8,128)(2,1)} fusion(bf16[8,128]{0,1:T(8,128)(2,1)S(1)} %copy.17, s32[16384]{0:T(1024)S(1)} %bitcast_clamp_fusion), kind=kCustom, calls=%fused_computation.1.clone | custom fusion | bytes 589824 | tf_op jit(solution)/shard_map/jit(_take)/gather | solution.py:49
  67.1 3.6 copy.20
  70.8 0.1 fusion.30
  70.9 1.1 fusion.1
  72.0 1.8 collective-permute-start
  73.8 57.4 %gather_fusion = bf16[16384,8]{1,0:T(8,128)(2,1)} fusion(bf16[8,128]{0,1:T(8,128)(2,1)S(1)} %copy.17, s32[16384]{0:T(1024)S(1)} %bitcast_clamp_fusion.1), kind=kCustom, calls=%fused_computation.clone | custom fusion | bytes 589824 | tf_op jit(solution)/shard_map/jit(_take)/gather | solution.py:49
  131.2 3.6 copy.18
  134.7 0.1 fusion.27
  134.8 0.3 convolution_bitcast_fusion
  135.1 0.1 bitcast_convert_fusion
  135.2 0.4 fusion
  135.6 2.1 copy.21
  137.7 2.8 convolution_convert_fusion.3
  140.5 3.1 convolution_convert_fusion.2
  143.6 0.0 all-reduce.5.cloned.1.call-update
  143.6 0.0 reduce-scatter.2.cloned.1.call-start
  143.6 85.0 %all-reduce.5.cloned.1.call-done = (bf16[256,512]{1,0:T(8,128)(2,1)}, bf16[256,512]{1,0:T(8,128)(2,1)}) async-done(((bf16[256,512]{1,0:T(8,128)(2,1)}, bf16[256,512]{1,0:T(8,128)(2,1)}), (bf16[256,512]{1,0:T(8,128)(2,1)}, bf16[256,512]{1,0:T(8,128)(2,1)})) %all-reduce.5.cloned.1.call-update) | async-done | bytes 524304 | tf_op jit(solution)/shard_map/psum | solution.py:83
  228.7 3.2 convolution_convert_fusion
  232.0 59.8 %reduce-scatter.2.cloned.1.call-done = bf16[128,512]{1,0:T(8,128)(2,1)} async-done(((bf16[2048,512]{1,0:T(8,128)(2,1)}), bf16[128,512]{1,0:T(8,128)(2,1)}) %reduce-scatter.2.cloned.1.call-update) | async-done | bytes 131088 | tf_op jit(solution)/shard_map/reduce_scatter | solution.py:87
  291.8 1.0 multiply_reduce_fusion.1
  292.8 18.1 %all-reduce.1 = (f32[512]{0:T(512)S(1)}, f32[512]{0:T(512)S(1)}) all-reduce(f32[512]{0:T(512)S(1)} %multiply_reduce_fusion.2, f32[512]{0:T(512)S(1)} %multiply_reduce_fusion.1), channel_id=1, replica_groups=mesh['tm'=16,'nin'=8,'nout'=4] {'nin'}, use_global_device_ids=true, to_apply=%region_1.2 | all-reduce | flops 1024 | bytes 8192 | tf_op jit(solution)/shard_map/psum | solution.py:15
  310.8 23.5 %all-reduce = (f32[512]{0:T(512)S(1)}, f32[512]{0:T(512)S(1)}) all-reduce(f32[512]{0:T(512)S(1)} %get-tuple-element.6, f32[512]{0:T(512)S(1)} %get-tuple-element.7), channel_id=1, replica_groups=mesh['tm'=16,'nin'=8,'nout'=4] {'tm'}, use_global_device_ids=true, to_apply=%region_2.3 | all-reduce | flops 1024 | bytes 8192 | tf_op jit(solution)/shard_map/psum | solution.py:15
  334.4 1.7 multiply_reduce_fusion
  336.1 246.9 %psum.55 = f32[512]{0:T(512)S(1)} all-reduce(f32[512]{0:T(512)S(1)} %get-tuple-element.10), channel_id=1, replica_groups=mesh['tm'=16,'nin'=8,'nout'=4] {'tm','nin'}, use_global_device_ids=true, to_apply=%region_11.13 | all-reduce | flops 512 | bytes 4096 | tf_op jit(solution)/shard_map/psum | solution.py:103
  583.0 0.8 multiply_add_fusion
  (29 shorter events, 0.2 us)
Async XLA Ops:
  7.2 130.6 %copy-start = (bf16[2048,512]{1,0:T(8,128)(2,1)S(1)}, bf16[2048,512]{1,0:T(8,128)(2,1)}, u32[]{:S(2)}) copy-start(bf16[2048,512]{1,0:T(8,128)(2,1)} %param.10) | copy-start | bytes 6291460
  7.2 133.3 %all-gather.2.cloned.1.call-start = ((), (), s32[]{:S(2)}) async-start(), calls=%async_computation.1 | async-start | bytes 2228224 | tf_op jit(solution)/shard_map/all_gather | solution.py:76
  9.0 219.6 %all-reduce.5.cloned.1.call-start = ((), (), s32[]{:S(2)}) async-start(), calls=%async_computation.3 | async-start | bytes 1048576 | tf_op jit(solution)/shard_map/psum | solution.py:83
  67.1 3.6 copy-start.5
  72.0 63.1 %collective-permute-start = (bf16[128,256,8]{1,0,2:T(8,128)(2,1)}, bf16[128,256,8]{1,0,2:T(8,128)(2,1)S(1)}, u32[]{:S(2)}, u32[]{:S(2)}) collective-permute-start(bf16[128,256,8]{1,0,2:T(8,128)(2,1)} %fusion.1), channel_id=1, source_target_pairs={{0,32},{32,64},{64,96},{96,128},{128,160},{160,192},{192,224},{224... | collective-permute-start | bytes 1572872 | tf_op jit(solution)/shard_map/ppermute | solution.py:25
  137.7 2.8 copy-start.2
  140.5 3.1 copy-start.7
  143.6 148.2 %reduce-scatter.2.cloned.1.call-start = ((), (), s32[]{:S(2)}) async-start(), calls=%async_computation.2 | async-start | bytes 2228224 | tf_op jit(solution)/shard_map/reduce_scatter | solution.py:87
  228.7 3.3 copy-start.4
  231.9 59.9 %copy-start.1 = (f32[128,512]{1,0:T(8,128)S(1)}, f32[128,512]{1,0:T(8,128)}, u32[]{:S(2)}) copy-start(f32[128,512]{1,0:T(8,128)} %param.11) | copy-start | bytes 786436
  231.9 102.5 %copy-start.6 = (f32[128,512]{1,0:T(8,128)S(1)}, f32[128,512]{1,0:T(8,128)}, u32[]{:S(2)}) copy-start(f32[128,512]{1,0:T(8,128)} %param.13) | copy-start | bytes 786436
  336.1 247.7 %copy-start.3 = (f32[128,512]{1,0:T(8,128)}, f32[128,512]{1,0:T(8,128)S(1)}, u32[]{:S(2)}) copy-start(f32[128,512]{1,0:T(8,128)S(1)} %get-tuple-element.11) | copy-start | bytes 786436
Sparse Core Ops, SparseCore 0:
  10.7 46.5 all-gather.1
  143.7 84.9 all-reduce.4
  232.0 59.6 reduce-scatter.1
